TPU v7x, 256 devices: a whole 4x4x8 slice. The times are simulated.
256 devices in a mesh: grp: 8 (over z_hi, core), tile: 32 (over x, y, z_lo).
Axes of the slice: x: 4, y: 4, z: 8 (z_hi: 4, z_lo: 2; z = z_hi * 2 + z_lo), core: 2. Of those that a mesh axis runs over, the one named last changes fastest.
Arguments:
- right_side: float32 [256, 16384], P('grp', 'tile'), may hold values from -8 to 8
- diagonal: float32 [256, 16384], P('grp', 'tile'), may hold values from 0.25 to 2
- inverse_factor: float32 [16384, 16384], P(('grp', 'tile')), may hold values from -2 to 2, as said below
Outputs:
- solution_field: float32 [256, 16384], P('grp', 'tile')
Inputs may be any that keep to these rules, and one draw needn't show every extreme that they name: `inverse_factor`: zero above the diagonal; the diagonal lies between 1 and 2.
All inputs are finite; a program needn't handle non-finite values.
Results may differ from a plain program's by a relative error of at most 0.0003.
Values sent between devices are 32-bit elements; how exact they have to be, the bound alone decides.
A program may use at most 64 MiB of HBM per device.

v0:
```python
import jax
import jax.numpy as jnp
from jax import lax
from jax.sharding import PartitionSpec as P

FAC = 16
SWEEPS = 4
CYCLES = 2


def extended(block, sides, width):
    for axis, dim in sides:
        count = lax.axis_size(axis)
        forward = [(i, i + 1) for i in range(count - 1)]
        backward = [(target, source) for source, target in forward]
        low = lax.ppermute(
            lax.slice_in_dim(block, block.shape[dim] - width, None, axis=dim), axis, forward
        )
        high = lax.ppermute(lax.slice_in_dim(block, 0, width, axis=dim), axis, backward)
        block = jnp.concatenate([low, block, high], axis=dim)
    return block


def operate(field, diagonal):
    padded = extended(field, (("grp", 0), ("tile", 1)), 1)
    beside = padded[2:, 1:-1] + padded[:-2, 1:-1] + padded[1:-1, 2:] + padded[1:-1, :-2]
    beside = beside + padded[2:, :-2] + padded[:-2, 2:]
    return (6.0 + diagonal) * field - beside


def shards(right_side, diagonal, inverse_factor):
    rows_here, cols_here = right_side.shape
    coarse_here = inverse_factor.shape[0]
    scale = 1.0 / (6.0 + diagonal)
    solution_field = jnp.zeros_like(right_side)
    for cycle in range(CYCLES):
        if cycle == 0:
            residual = right_side
        else:
            residual = right_side - operate(solution_field, diagonal)
        smoothed = None
        coarse_rhs = jnp.mean(
            residual.reshape(rows_here // FAC, FAC, cols_here // FAC, FAC), axis=(1, 3)
        ).reshape(-1)
        inner = jnp.dot(
            inverse_factor,
            lax.all_gather(coarse_rhs, ("grp", "tile"), axis=0, tiled=True),
            precision=lax.Precision.HIGHEST,
        )
        smoothed = 0.8 * residual * scale
        for sweep in range(SWEEPS - 1):
            smoothed = smoothed + 0.8 * (residual - operate(smoothed, diagonal)) * scale
        whole_term = jnp.dot(inner, inverse_factor, precision=lax.Precision.HIGHEST)
        summed = lax.psum(whole_term, ("grp", "tile"))
        offset = lax.axis_index(("grp", "tile")) * coarse_here
        coarse_fix = lax.dynamic_slice_in_dim(summed, offset, coarse_here, 0)
        blocks = coarse_fix.reshape(rows_here // FAC, 1, cols_here // FAC, 1)
        spread_fix = jnp.broadcast_to(
            blocks, (rows_here // FAC, FAC, cols_here // FAC, FAC)
        ).reshape(rows_here, cols_here)
        solution_field = solution_field + smoothed + 0.5 * spread_fix
    return solution_field


def solution(mesh):
    placed = (P("grp", "tile"), P("grp", "tile"), P(("grp", "tile"), None))
    return jax.shard_map(
        shards, mesh=mesh, in_specs=placed, out_specs=P("grp", "tile"), check_vma=False
    )
```

profile of v0, /device:TPU:1, one launch (start us, length us, event | category | flops | bytes accessed | tf_op | source)
XLA Modules:
  0.0 1096.1 jit_solution(2937678232551976307)
XLA Ops:
  7.4 5.1 collective-permute-start
  12.6 3.1 collective-permute-start.1
  16.5 3.5 collective-permute-start.3
  21.3 3.2 collective-permute-done.2
  25.6 1.9 collective-permute-start.4
  27.6 6.5 collective-permute-start.5
  35.2 3.7 collective-permute-start.7
  40.4 3.1 collective-permute-done.6
  44.6 1.9 collective-permute-start.8
  46.5 6.2 collective-permute-start.9
  53.8 3.5 collective-permute-start.11
  58.6 239.1 %all-reduce.11.cloned.1.call-done = f32[16384]{0:T(1024)} async-done(((f32[16384]{0:T(1024)}), f32[16384]{0:T(1024)}) %all-reduce.11.cloned.1.call-update) | async-done | bytes 65552
  297.8 5.7 convolution_bitcast_fusion.1
  303.5 2.7 fusion.50
  306.4 234.0 %all-reduce.7.cloned.1.call-done = f32[16384]{0:T(1024)} async-done(((f32[16384]{0:T(1024)}), f32[16384]{0:T(1024)}) %all-reduce.7.cloned.1.call-update) | async-done | bytes 65552 | tf_op jit(solution)/shard_map/psum | solution.py:54
  541.8 1.9 collective-permute-start.12
  543.7 4.5 collective-permute-start.13
  549.1 3.7 collective-permute-start.15
  554.0 3.2 collective-permute-done.14
  557.5 1.9 collective-permute-start.16
  559.4 6.5 collective-permute-start.17
  566.7 2.8 collective-permute-start.19
  570.8 3.2 collective-permute-done.18
  576.2 6.5 collective-permute-start.21
  583.5 3.5 collective-permute-start.23
  588.5 3.1 collective-permute-done.22
  593.7 6.6 collective-permute-start.25
  601.5 3.1 collective-permute-start.27
  606.1 238.9 %all-reduce.13.cloned.1.call-done = f32[16384]{0:T(1024)} async-done(((f32[16384]{0:T(1024)}), f32[16384]{0:T(1024)}) %all-reduce.13.cloned.1.call-update) | async-done | bytes 65552
  844.9 5.7 convolution_bitcast_fusion
  850.6 2.7 fusion.51
  853.5 234.1 %all-reduce.9.cloned.1.call-done = f32[16384]{0:T(1024)} async-done(((f32[16384]{0:T(1024)}), f32[16384]{0:T(1024)}) %all-reduce.9.cloned.1.call-update) | async-done | bytes 65552 | tf_op jit(solution)/shard_map/psum | solution.py:54
  (101 shorter events, 27.1 us)
Async XLA Ops:
  6.5 291.2 %all-reduce.11.cloned.1.call-start = ((), (), s32[]{:S(2)}) async-start(), calls=%async_computation.2 | async-start | bytes 131072
  7.4 8.2 collective-permute-start
  12.6 3.8 collective-permute-start.1
  16.5 4.8 collective-permute-start.3
  20.0 4.5 collective-permute-start.2
  25.6 9.5 collective-permute-start.4
  27.6 7.6 collective-permute-start.5
  35.2 5.1 collective-permute-start.7
  38.9 4.5 collective-permute-start.6
  44.6 9.1 collective-permute-start.8
  46.5 7.2 collective-permute-start.9
  53.7 486.7 %all-reduce.7.cloned.1.call-start = ((), (), s32[]{:S(2)}) async-start(), calls=%async_computation | async-start | bytes 131072 | tf_op jit(solution)/shard_map/psum | solution.py:54
  53.8 252.4 %collective-permute-start.11 = (f32[34,1]{1,0:T(8,128)S(1)}, f32[34,1]{1,0:T(8,128)S(1)}, u32[]{:S(2)}, u32[]{:S(2)}) collective-permute-start(f32[34,1]{1,0:T(8,128)S(1)} %get-tuple-element.25), channel_id=1, source_target_pairs={{0,1},{1,2},{2,3},{3,4},{4,5},{5,6},{6,7},{7,8},{8,9},{9,10},{10,1... | collective-permute-start | bytes 416 | tf_op jit(solution)/shard_map/ppermute | solution.py:16
  57.3 249.0 %collective-permute-start.10 = (f32[34,1]{1,0:T(8,128)S(1)}, f32[34,1]{1,0:T(8,128)S(1)}, u32[]{:S(2)}, u32[]{:S(2)}) collective-permute-start(f32[34,1]{1,0:T(8,128)S(1)} %get-tuple-element.26), channel_id=1, source_target_pairs={{1,0},{2,1},{3,2},{4,3},{5,4},{6,5},{7,6},{8,7},{9,8},{10,9},{11,1... | collective-permute-start | bytes 416 | tf_op jit(solution)/shard_map/ppermute | solution.py:19
  306.2 538.7 %all-reduce.13.cloned.1.call-start = ((), (), s32[]{:S(2)}) async-start(), calls=%async_computation.3 | async-start | bytes 131072
  541.8 6.5 collective-permute-start.12
  543.7 5.3 collective-permute-start.13
  549.1 5.0 collective-permute-start.15
  552.7 4.5 collective-permute-start.14
  557.5 8.5 collective-permute-start.16
  559.4 7.2 collective-permute-start.17
  566.7 4.1 collective-permute-start.19
  569.5 4.5 collective-permute-start.18
  574.3 8.7 collective-permute-start.20
  576.2 7.2 collective-permute-start.21
  583.5 5.0 collective-permute-start.23
  587.0 4.5 collective-permute-start.22
  591.8 9.6 collective-permute-start.24
  593.7 7.7 collective-permute-start.25
  601.4 486.2 %all-reduce.9.cloned.1.call-start = ((), (), s32[]{:S(2)}) async-start(), calls=%async_computation.1 | async-start | bytes 131072 | tf_op jit(solution)/shard_map/psum | solution.py:54
  601.5 251.9 %collective-permute-start.27 = (f32[34,1]{1,0:T(8,128)S(1)}, f32[34,1]{1,0:T(8,128)S(1)}, u32[]{:S(2)}, u32[]{:S(2)}) collective-permute-start(f32[34,1]{1,0:T(8,128)S(1)} %get-tuple-element.9), channel_id=1, source_target_pairs={{0,1},{1,2},{2,3},{3,4},{4,5},{5,6},{6,7},{7,8},{8,9},{9,10},{10,1... | collective-permute-start | bytes 416 | tf_op jit(solution)/shard_map/ppermute | solution.py:16
  604.6 248.8 %collective-permute-start.26 = (f32[34,1]{1,0:T(8,128)S(1)}, f32[34,1]{1,0:T(8,128)S(1)}, u32[]{:S(2)}, u32[]{:S(2)}) collective-permute-start(f32[34,1]{1,0:T(8,128)S(1)} %get-tuple-element.10), channel_id=1, source_target_pairs={{1,0},{2,1},{3,2},{4,3},{5,4},{6,5},{7,6},{8,7},{9,8},{10,9},{11,1... | collective-permute-start | bytes 416 | tf_op jit(solution)/shard_map/ppermute | solution.py:19
  (6 other events, 500.5 us)
Sparse Core Ops, SparseCore 0:
  53.8 243.9 all-reduce.10
  306.3 234.0 all-reduce.6
  601.5 243.4 all-reduce.12
  853.5 234.0 all-reduce.8
where the time goes:
time: 1100 us
  waiting for transfers between devices  965 us (88%)
  starting transfers between devices  89.7 us (8%)
  matrix products  16.9 us (2%)
  between operations  13.7 us (1%)
    unnamed x6, waiting for transfers between devices  478 us
    psum x2, waiting for transfers between devices, shards(): summed = lax.psum(whole_term, ('grp', 'tile'))  468 us
    ppermute x14, starting transfers between devices, extended(): lax.ppermute(lax.slice_in_dim(block, block.shape[dim] - width, None, axis...  63.7 us
    ppermute x14, starting transfers between devices, extended(): lax.ppermute(lax.slice_in_dim(block, 0, width, axis=dim), axis, backward)  25.9 us
  transfers between devices with their start and end apart: 32, of which 13 were waited for; matrix products, arithmetic and copies ran while one was open for 2% of the time, Pallas kernels for 0%

commit v1 on v0

--- a/solution.py
+++ b/solution.py
@@ -51,7 +51,8 @@
         for sweep in range(SWEEPS - 1):
             smoothed = smoothed + 0.8 * (residual - operate(smoothed, diagonal)) * scale
         whole_term = jnp.dot(inner, inverse_factor, precision=lax.Precision.HIGHEST)
-        summed = lax.psum(whole_term, ("grp", "tile"))
+        pieces = lax.all_gather(whole_term, ("grp", "tile"), axis=0, tiled=False)
+        summed = pieces.sum(axis=0)
         offset = lax.axis_index(("grp", "tile")) * coarse_here
         coarse_fix = lax.dynamic_slice_in_dim(summed, offset, coarse_here, 0)
         blocks = coarse_fix.reshape(rows_here // FAC, 1, cols_here // FAC, 1)

time: 1100 us -> 2050 us (1.86)
  waiting for transfers between devices: 965 us -> 1870 us
  local copies, waits for them, and re-layouts: 4.15 us -> 40.6 us
    all_gather x0 -> x2, waiting for transfers between devices: none -> 1350 us  [shards(): pieces = lax.all_gather(whole_term, ('grp', 'tile'), axis=0, tiled=False)]
    psum x2 -> x0, waiting for transfers between devices: 468 us -> none  [shards(): summed = lax.psum(whole_term, ('grp', 'tile'))]
    all_gather x0 -> x2, local copies, waits for them, and re-layouts: none -> 36.4 us  [shards(): pieces = lax.all_gather(whole_term, ('grp', 'tile'), axis=0, tiled=False)]
  transfers between devices with their start and end apart: 32 -> 32, of which waited for: 13 -> 18; matrix products, arithmetic and copies ran while one was open for 2% -> 0% of each run, Pallas kernels for 0% -> 0%
where the time goes in v1:
time: 2050 us
  waiting for transfers between devices  1870 us (91%)
  starting transfers between devices  89.1 us (4%)
  local copies, waits for them, and re-layouts  40.6 us (2%)
    all_gather x2, waiting for transfers between devices, shards(): pieces = lax.all_gather(whole_term, ('grp', 'tile'), axis=0, tiled=False)  1350 us
    unnamed x6, waiting for transfers between devices  486 us
    ppermute x14, starting transfers between devices, extended(): lax.ppermute(lax.slice_in_dim(block, block.shape[dim] - width, None, axis...  65.4 us
  transfers between devices with their start and end apart: 32, of which 18 were waited for; matrix products, arithmetic and copies ran while one was open for 0% of the time, Pallas kernels for 0%

profile of v1, /device:TPU:1, one launch (start us, length us, event | category | flops | bytes accessed | tf_op | source)
XLA Modules:
  0.0 2046.4 jit_solution(17362660020057242570)
XLA Ops:
  8.8 246.0 %all-reduce.5.cloned.1.call-done = f32[16384]{0:T(1024)} async-done(((f32[16384]{0:T(1024)}), f32[16384]{0:T(1024)}) %all-reduce.5.cloned.1.call-update) | async-done | bytes 65552
  254.8 5.7 convolution_bitcast_fusion.1
  265.3 4.5 collective-permute-start.1
  270.6 3.7 collective-permute-start.3
  275.6 3.8 collective-permute-done.2
  281.5 6.0 collective-permute-start.5
  288.3 2.8 collective-permute-start.7
  292.4 3.6 collective-permute-done.6
  298.2 6.1 collective-permute-start.9
  305.1 3.7 collective-permute-start.11
  310.1 3.2 collective-permute-done.10
  313.4 677.3 %all-gather.5.cloned.1.call-done = f32[4194304]{0:T(1024)} async-done(((f32[16384]{0:T(1024)}), f32[4194304]{0:T(1024)}) %all-gather.5.cloned.1.call-update) | async-done | bytes 16777232 | tf_op jit(solution)/shard_map/all_gather | solution.py:54
  990.7 18.2 reshape.30
  1008.9 6.6 reduce_sum.37
  1016.2 2.8 collective-permute-start.12
  1019.1 6.5 collective-permute-start.13
  1026.4 5.0 collective-permute-start.15
  1032.7 3.2 collective-permute-done.14
  1037.7 240.1 %all-reduce.7.cloned.1.call-done = f32[16384]{0:T(1024)} async-done(((f32[16384]{0:T(1024)}), f32[16384]{0:T(1024)}) %all-reduce.7.cloned.1.call-update) | async-done | bytes 65552
  1277.8 5.7 convolution_bitcast_fusion
  1288.2 4.5 collective-permute-start.17
  1293.5 3.7 collective-permute-start.19
  1298.5 3.8 collective-permute-done.18
  1304.4 6.0 collective-permute-start.21
  1311.2 2.8 collective-permute-start.23
  1315.3 3.2 collective-permute-done.22
  1320.7 6.5 collective-permute-start.25
  1328.0 3.7 collective-permute-start.27
  1333.0 3.3 collective-permute-done.26
  1336.5 677.3 %all-gather.7.cloned.1.call-done = f32[4194304]{0:T(1024)} async-done(((f32[16384]{0:T(1024)}), f32[4194304]{0:T(1024)}) %all-gather.7.cloned.1.call-update) | async-done | bytes 16777232 | tf_op jit(solution)/shard_map/all_gather | solution.py:54
  2013.8 18.2 reshape.31
  2032.0 6.6 reduce_sum.39
  (105 shorter events, 38.6 us)
Async XLA Ops:
  6.5 248.2 %all-reduce.5.cloned.1.call-start = ((), (), s32[]{:S(2)}) async-start(), calls=%async_computation.2 | async-start | bytes 131072
  8.7 982.0 %all-gather.5.cloned.1.call-start = ((), (), s32[]{:S(2)}) async-start(), calls=%async_computation | async-start | bytes 16842752 | tf_op jit(solution)/shard_map/all_gather | solution.py:54
  263.2 1014.6 %all-reduce.7.cloned.1.call-start = ((), (), s32[]{:S(2)}) async-start(), calls=%async_computation.3 | async-start | bytes 131072
  263.3 6.5 collective-permute-start
  265.3 5.3 collective-permute-start.1
  270.6 5.0 collective-permute-start.3
  274.3 5.1 collective-permute-start.2
  279.6 7.9 collective-permute-start.4
  281.5 6.7 collective-permute-start.5
  288.3 4.1 collective-permute-start.7
  291.1 4.9 collective-permute-start.6
  296.2 8.0 collective-permute-start.8
  298.2 6.8 collective-permute-start.9
  305.1 5.0 collective-permute-start.11
  308.8 4.6 collective-permute-start.10
  1016.2 9.4 collective-permute-start.12
  1019.1 7.2 collective-permute-start.13
  1026.4 6.3 collective-permute-start.15
  1031.4 4.5 collective-permute-start.14
  1037.5 976.3 %all-gather.7.cloned.1.call-start = ((), (), s32[]{:S(2)}) async-start(), calls=%async_computation.1 | async-start | bytes 16842752 | tf_op jit(solution)/shard_map/all_gather | solution.py:54
  1286.3 6.5 collective-permute-start.16
  1288.2 5.3 collective-permute-start.17
  1293.5 5.0 collective-permute-start.19
  1297.2 5.1 collective-permute-start.18
  1302.5 7.9 collective-permute-start.20
  1304.4 6.7 collective-permute-start.21
  1311.2 4.1 collective-permute-start.23
  1314.0 4.5 collective-permute-start.22
  1318.8 8.5 collective-permute-start.24
  1320.7 7.2 collective-permute-start.25
  1328.0 5.0 collective-permute-start.27
  1331.7 4.6 collective-permute-start.26
  (6 other events, 29.7 us)
Sparse Core Ops, SparseCore 0:
  12.9 241.8 all-reduce.4
  263.3 727.3 all-gather.4
  1037.6 240.1 all-reduce.6
  1286.4 727.3 all-gather.6
